TPU v7x, 256 devices: a whole 4x4x8 slice. The times are simulated.
256 devices in a mesh: section: 4 (over x_hi, core), expert: 64 (over x_lo, y, z).
Axes of the slice: x: 4 (x_hi: 2, x_lo: 2; x = x_hi * 2 + x_lo), y: 4, z: 8, core: 2. Of those that a mesh axis runs over, the one named last changes fastest.
Arguments:
- layer_input: bfloat16 [2, 4, 8192, 2048], P(None, 'section', 'expert'), may hold values from -48 to 48
- entering: bfloat16 [4, 8192, 2048], P('section', 'expert'), may hold values from -6 to 6
- fresh: bfloat16 [1, 8192, 2048], P(None, 'expert'), may hold values from -6 to 6
- routes: int32 [2, 4, 8192, 2], P(None, 'section', 'expert'), may hold values from 0 to 63, all different within a row; in each aligned block of 128 rows (0 to 127, 128 to 255, ..., all dimensions but the last counted through in order) at most 6 rows name the same one
- gate_weights: bfloat16 [2, 4, 8192, 2], P(None, 'section', 'expert'), may hold values from 0.019897461 to 0.5
- norm_gain: float32 [4, 2048], P('section'), may hold values from 0.3 to 3
- w_gate: bfloat16 [4, 64, 2048, 768], P('section', 'expert'), may hold values from -0.125 to 0.125
- w_up: bfloat16 [4, 64, 2048, 768], P('section', 'expert'), may hold values from -0.125 to 0.125
- w_down: bfloat16 [4, 64, 768, 2048], P('section', 'expert'), may hold values from -0.21875 to 0.21875
Outputs:
- produced: bfloat16 [2, 4, 8192, 2048], P(None, 'section', 'expert')
Inputs may be any that keep to these rules, and one draw needn't show every extreme that they name: `routes`: each row names 2 different experts; in each aligned block of 128 rows no expert is named more than 6 times, a bound that some block reaches.
All inputs are finite; a program needn't handle non-finite values.
Results may differ from a plain program's by a relative error of at most 0.0052.
Values may be sent and summed in bfloat16 or wider, within the bound.
A program may use at most 128 MiB of HBM per device.

v0:
```python
import jax
import jax.numpy as jnp
from jax import lax
from jax.sharding import PartitionSpec as P

D = 2048
TOPK = 2
EXP_DEV = 1
TICKS = 2
TOK_DEV = 128


def in_one_piece(arrays, axis, split_dim, concat_dim, along):
    columns = [a.reshape(*a.shape[:along], -1) for a in arrays]
    both = jnp.concatenate(columns, axis=along)
    whole, at, outs = (
        lax.all_to_all(both, axis, split_axis=split_dim, concat_axis=concat_dim, tiled=True),
        0,
        [],
    )
    for a, column in zip(arrays, columns):
        share = whole[..., at : at + column.shape[along]]
        outs.append(share.reshape(*share.shape[:along], *a.shape[along:]))
        at += column.shape[along]
    return tuple(outs)


def from_behind(x, axis, by):
    length = lax.axis_size(axis)
    pairs = [(i, i + by) for i in range(length) if 0 <= i + by < length]
    return lax.ppermute(x, axis, pairs)


def contract_last(left, right):
    return lax.dot_general(
        left, right, (((1,), (1,)), ((), ())), preferred_element_type=jnp.float32
    )


def expert_backward(normed_rows, scaled_rows, gate_matrix, up_matrix, down_matrix):
    pre_gate = jnp.dot(normed_rows, gate_matrix, preferred_element_type=jnp.float32)
    pre_up = jnp.dot(normed_rows, up_matrix, preferred_element_type=jnp.float32)
    hidden_grad = contract_last(scaled_rows, down_matrix)
    sigmoid = jax.nn.sigmoid(pre_gate)
    gate_grad = (hidden_grad * pre_up * sigmoid * (1.0 + pre_gate * (1.0 - sigmoid))).astype(
        jnp.bfloat16
    )
    up_grad = (hidden_grad * pre_gate * sigmoid).astype(jnp.bfloat16)
    summed = contract_last(gate_grad, gate_matrix) + contract_last(up_grad, up_matrix)
    return summed.astype(jnp.bfloat16)


def expert_side(normed_in, grads_in, gates_in, w_gate, w_up, w_down):
    sources, local_count, slot_width, model_width = normed_in.shape
    normed_rows = normed_in[:, 0].reshape(-1, model_width)
    grad_rows = grads_in[:, 0].reshape(-1, model_width)
    gate_rows = gates_in[:, 0].reshape(-1)
    scaled_rows = (gate_rows.astype(jnp.float32)[:, None] * grad_rows.astype(jnp.float32)).astype(
        jnp.bfloat16
    )
    gate_matrix = w_gate[0, 0]
    up_matrix = w_up[0, 0]
    down_matrix = w_down[0, 0]
    result = expert_backward(normed_rows, scaled_rows, gate_matrix, up_matrix, down_matrix)
    outputs = [result.reshape(sources, slot_width, model_width)]
    return jnp.stack(outputs, axis=1)


def place_slots(values, slot_flat, devices_expert, slot_count):
    buffer = (
        jnp.zeros((devices_expert * EXP_DEV * slot_count,) + values.shape[1:], values.dtype)
        .at[slot_flat]
        .set(values)
    )
    return buffer.reshape((devices_expert, EXP_DEV, slot_count) + values.shape[1:])


def local(layer_input, entering, fresh, routes, gate_weights, norm_gain, w_gate, w_up, w_down):
    devices_expert = lax.axis_size("expert")
    experts_all = EXP_DEV * devices_expert
    slot_count = max(2, min(TOK_DEV, 3 * TOK_DEV * TOPK // (2 * experts_all)))
    section_last = lax.axis_size("section") - 1
    section_here = lax.axis_index("section")
    gain_row = norm_gain[0]
    token_of = jnp.arange(TOK_DEV * TOPK, dtype=jnp.int32) // TOPK
    expert_ids = jnp.arange(experts_all, dtype=jnp.int32)
    slot_table = []
    normed_table = []
    inverse_table = []
    for step_index in range(TICKS):
        flat_routes = routes[step_index, 0].reshape(-1)
        onehot = (flat_routes[:, None] == expert_ids[None, :]).astype(jnp.int32)
        earlier = jnp.cumsum(onehot, axis=0) - onehot
        rank_within = jnp.sum(earlier * onehot, axis=1)
        slot_table.append(flat_routes * slot_count + rank_within)
        xfloat = layer_input[step_index, 0].astype(jnp.float32)
        inverse = lax.rsqrt(jnp.mean(xfloat * xfloat, axis=1, keepdims=True) + 1e-05)
        inverse_table.append(inverse)
        normed_table.append((xfloat * inverse * gain_row).astype(jnp.bfloat16))
    normed_all = jnp.stack(
        [
            place_slots(
                normed_table[step_index][token_of],
                slot_table[step_index],
                devices_expert,
                slot_count,
            )
            for step_index in range(TICKS)
        ],
        axis=0,
    )
    normed_far = lax.all_to_all(normed_all, "expert", split_axis=1, concat_axis=1, tiled=True)
    results = []
    arrived = entering[0]
    for step_index in range(TICKS):
        if step_index == 0:
            incoming = entering[0]
        else:
            incoming = jnp.where(section_here == section_last, fresh[step_index - 1], arrived)
        slot_flat = slot_table[step_index]
        grads_packed = place_slots(incoming[token_of], slot_flat, devices_expert, slot_count)
        gates_packed = place_slots(
            gate_weights[step_index, 0].reshape(-1), slot_flat, devices_expert, slot_count
        )
        grads_far, gates_far = in_one_piece((grads_packed, gates_packed), "expert", 0, 0, 3)
        computed = expert_side(normed_far[step_index], grads_far, gates_far, w_gate, w_up, w_down)
        returned = lax.all_to_all(computed, "expert", split_axis=0, concat_axis=0, tiled=True)
        picked = jnp.take(returned.reshape(experts_all * slot_count, D), slot_flat, axis=0)
        normed_grad = jnp.sum(picked.reshape(TOK_DEV, TOPK, D).astype(jnp.float32), axis=1)
        xfloat = layer_input[step_index, 0].astype(jnp.float32)
        inverse = inverse_table[step_index]
        weighted = gain_row * normed_grad
        project = jnp.mean(xfloat * weighted, axis=1, keepdims=True)
        result = (
            incoming.astype(jnp.float32) + inverse * weighted - xfloat * inverse**3 * project
        ).astype(jnp.bfloat16)
        results.append(result)
        if step_index + 1 < TICKS:
            arrived = from_behind(result, "section", -1)
    return jnp.stack(results, axis=0)[:, None]


def solution(mesh):
    in_specs = (
        P(None, "section", "expert", None),
        P("section", "expert", None),
        P(None, "expert", None),
        P(None, "section", "expert", None),
        P(None, "section", "expert", None),
        P("section", None),
        P("section", "expert", None, None),
        P("section", "expert", None, None),
        P("section", "expert", None, None),
    )
    out_specs = P(None, "section", "expert", None)
    return jax.shard_map(local, mesh=mesh, in_specs=in_specs, out_specs=out_specs, check_vma=False)
```

profile of v0, /device:TPU:1, one launch (start us, length us, event | category | flops | bytes accessed | tf_op | source)
XLA Modules:
  0.0 481.1 jit_solution(14198050225875093850)
XLA Ops:
  2.5 6.8 %scatter_custom_fusion = bf16[384,2048]{1,0:T(8,128)(2,1)} fusion(s32[256]{0:T(256)S(1)} %bitcast.197, bf16[128,2048]{1,0:T(8,128)(2,1)} %bitcast.185, s32[1024]{0:T(1024)S(1)} %pad_clamp_fusion.2, bf16[]{:T(256)} %constant.52.clone.1), kind=kCustom, calls=%fused_computation.93 | custom fusion | bytes 1573376 | tf_op jit(solution)/shard_map/scatter | solution.py:73
  19.3 14.5 %all-to-all-start = ((bf16[64,1,6,2049]{3,2,1,0:T(8,128)(2,1)}), bf16[64,1,6,2049]{3,2,1,0:T(8,128)(2,1)}, u32[]{:S(2)}, u32[]{:S(2)}) async-start(bf16[64,1,6,2049]{3,2,1,0:T(8,128)(2,1)} %maximum_bitcast_fusion), calls=%async_computation | async-start | bytes 4456448 | tf_op jit(solution)/shard_map/all_to_all | solution.py:17
  37.0 7.1 %scatter_custom_fusion.2 = bf16[384,2048]{1,0:T(8,128)(2,1)} fusion(s32[256]{0:T(256)S(1)} %bitcast.199, bf16[128,2048]{1,0:T(8,128)(2,1)} %get-tuple-element.14, s32[1024]{0:T(1024)S(1)} %pad_clamp_fusion.2, bf16[]{:T(256)} %constant.52.clone.1), kind=kCustom, calls=%fused_computation.91 | custom fusion | bytes 1573376 | tf_op jit(solution)/shard_map/scatter | solution.py:73
  49.0 7.0 %scatter_custom_fusion.3 = bf16[384,2048]{1,0:T(8,128)(2,1)} fusion(s32[256]{0:T(256)S(1)} %bitcast.194, bf16[128,2048]{1,0:T(8,128)(2,1)} %get-tuple-element.15, s32[1024]{0:T(1024)S(1)} %pad_clamp_fusion.2, bf16[]{:T(256)} %constant.52.clone.1), kind=kCustom, calls=%fused_computation.89 | custom fusion | bytes 1573376 | tf_op jit(solution)/shard_map/scatter | solution.py:73
  63.0 5.0 %copy.41 = bf16[2,64,1,6,2048]{4,0,3,2,1:T(2,128)(2,1)} copy(bf16[2,64,1,6,2048]{4,3,1,2,0:T(8,128)(2,1)S(1)} %pad_maximum_fusion) | data formatting | bytes 6291456 | tf_op jit(solution)/shard_map/stack | solution.py:100
  68.0 17.1 %all-to-all-done = bf16[64,1,6,2049]{3,2,1,0:T(8,128)(2,1)} async-done(((bf16[64,1,6,2049]{3,2,1,0:T(8,128)(2,1)}), bf16[64,1,6,2049]{3,2,1,0:T(8,128)(2,1)}, u32[]{:S(2)}, u32[]{:S(2)}) %all-to-all-start) | async-done | bytes 1573664 | tf_op jit(solution)/shard_map/all_to_all | solution.py:17
  85.1 8.0 %all-to-all-start.1 = ((bf16[2,64,1,6,2048]{4,0,3,2,1:T(2,128)(2,1)}), bf16[2,64,1,6,2048]{4,0,3,2,1:T(2,128)(2,1)}, u32[]{:S(2)}, u32[]{:S(2)}) async-start(bf16[2,64,1,6,2048]{4,0,3,2,1:T(2,128)(2,1)} %copy.41), calls=%async_computation.1 | async-start | bytes 6291456 | tf_op jit(solution)/shard_map/all_to_all | solution.py:112
  101.4 4.8 fusion.18
  106.2 56.2 %all-to-all-done.1 = bf16[2,64,1,6,2048]{4,0,3,2,1:T(2,128)(2,1)} async-done(((bf16[2,64,1,6,2048]{4,0,3,2,1:T(2,128)(2,1)}), bf16[2,64,1,6,2048]{4,0,3,2,1:T(2,128)(2,1)}, u32[]{:S(2)}, u32[]{:S(2)}) %all-to-all-start.1) | async-done | bytes 3145760 | tf_op jit(solution)/shard_map/all_to_all | solution.py:112
  162.4 17.4 %slice_reduce_fusion = (bf16[64,6,2048]{2,1,0:T(8,128)(2,1)}, bf16[64,6,2048]{2,1,0:T(8,128)(2,1)}) fusion(bf16[2,64,1,6,2048]{4,0,3,2,1:T(2,128)(2,1)} %all-to-all-done.1), kind=kLoop, calls=%fused_computation.15 | loop fusion | bytes 6291456 | tf_op jit(solution)/shard_map/slice | solution.py:126
  183.4 4.8 fusion.6
  188.2 7.8 %fusion.4 = f32[384,2048]{1,0:T(8,128)} fusion(bf16[1,1,2048,768]{3,2,1,0:T(8,128)(2,1)} %param.17, f32[384,768]{1,0:T(8,128)} %fusion.18, bf16[384,2048]{1,0:T(8,128)(2,1)} %reshape_squeeze_squeeze.6, bf16[1,1,2048,768]{3,2,1,0:T(8,128)(2,1)S(1)} %copy-done, f32[384,768]{1,0:T(8,128)} %fusion.6), kind=kOutput, calls=%fused_computation.21 | convolution fusion | flops 2418868224 | bytes 13369344 | tf_op jit(solution)/shard_map/dot_general | solution.py:35
  196.0 5.2 %add_convert_fusion.1 = bf16[384,2048]{1,0:T(8,128)(2,1)} fusion(f32[384,2048]{1,0:T(8,128)} %fusion.4, bf16[1,1,2048,768]{3,2,1,0:T(8,128)(2,1)S(1)} %copy-done, f32[384,768]{1,0:T(8,128)} %fusion.18, f32[384,768]{1,0:T(8,128)} %fusion.6), kind=kOutput, calls=%fused_computation.38 | convolution fusion | flops 1211301888 | bytes 10223616 | tf_op jit(solution)/shard_map/dot_general | solution.py:35
  204.9 9.7 %all-to-all-start.2 = ((bf16[64,1,6,2048]{3,2,1,0:T(8,128)(2,1)}), bf16[64,1,6,2048]{3,2,1,0:T(8,128)(2,1)}, u32[]{:S(2)}, u32[]{:S(2)}) async-start(bf16[64,1,6,2048]{3,2,1,0:T(8,128)(2,1)} %bitcast.184), calls=%async_computation.2 | async-start | bytes 4194304 | tf_op jit(solution)/shard_map/all_to_all | solution.py:127
  214.6 47.2 %all-to-all-done.2 = bf16[64,1,6,2048]{3,2,1,0:T(8,128)(2,1)} async-done(((bf16[64,1,6,2048]{3,2,1,0:T(8,128)(2,1)}), bf16[64,1,6,2048]{3,2,1,0:T(8,128)(2,1)}, u32[]{:S(2)}, u32[]{:S(2)}) %all-to-all-start.2) | async-done | bytes 1572896 | tf_op jit(solution)/shard_map/all_to_all | solution.py:127
  265.5 4.9 %gather_fusion = bf16[256,2048]{1,0:T(8,128)(2,1)} fusion(bf16[384,2048]{1,0:T(8,128)(2,1)} %reshape.338, s32[1024]{0:T(1024)S(1)} %pad_clamp_fusion.1), kind=kCustom, calls=%fused_computation.clone | custom fusion | bytes 2098176 | tf_op jit(solution)/shard_map/jit(_take)/gather | solution.py:128
  276.7 5.1 %reduce_sum.84 = f32[128,2048]{1,0:T(8,128)} reduce(f32[128,2,2048]{2,1,0:T(2,128)} %reshape.344, f32[]{:T(128)} %constant.49.clone.1), dimensions={1}, to_apply=%region_12.14 | reduce | flops 262144 | bytes 3145732 | tf_op jit(solution)/shard_map/reduce_sum | solution.py:129
  286.0 6.9 %collective-permute-start = (bf16[128,2048]{1,0:T(8,128)(2,1)}, bf16[128,2048]{1,0:T(8,128)(2,1)}, u32[]{:S(2)}, u32[]{:S(2)}) collective-permute-start(bf16[128,2048]{1,0:T(8,128)(2,1)} %fusion.58), channel_id=1, source_target_pairs={{64,0},{128,64},{192,128},{65,1},{129,65},{193,129},{66,2},{130,66... | collective-permute-start | bytes 1572872 | tf_op jit(solution)/shard_map/ppermute | solution.py:31
  296.1 6.4 %collective-permute-done = bf16[128,2048]{1,0:T(8,128)(2,1)} collective-permute-done((bf16[128,2048]{1,0:T(8,128)(2,1)}, bf16[128,2048]{1,0:T(8,128)(2,1)}, u32[]{:S(2)}, u32[]{:S(2)}) %collective-permute-start) | collective-permute-done | bytes 524320 | tf_op jit(solution)/shard_map/ppermute | solution.py:31
  304.5 7.0 %scatter_custom_fusion.4 = bf16[384,2048]{1,0:T(8,128)(2,1)} fusion(s32[256]{0:T(256)S(1)} %bitcast.196, bf16[128,2048]{1,0:T(8,128)(2,1)} %bitcast_select_fusion, s32[1024]{0:T(1024)S(1)} %pad_clamp_fusion.2, bf16[]{:T(256)} %constant.52.clone.1), kind=kCustom, calls=%fused_computation.87 | custom fusion | bytes 1573376 | tf_op jit(solution)/shard_map/scatter | solution.py:73
  318.7 6.0 %all-to-all-start.3 = ((bf16[64,1,6,2049]{3,2,1,0:T(8,128)(2,1)}), bf16[64,1,6,2049]{3,2,1,0:T(8,128)(2,1)}, u32[]{:S(2)}, u32[]{:S(2)}) async-start(bf16[64,1,6,2049]{3,2,1,0:T(8,128)(2,1)} %maximum_bitcast_fusion.1), calls=%async_computation.3 | async-start | bytes 4456448 | tf_op jit(solution)/shard_map/all_to_all | solution.py:17
  324.7 3.7 reshape_squeeze_squeeze.7
  328.4 4.8 %fusion.2 = f32[384,768]{1,0:T(8,128)} fusion(bf16[384,2048]{1,0:T(8,128)(2,1)} %reshape_squeeze_squeeze.7, bf16[1,1,2048,768]{3,2,1,0:T(8,128)(2,1)} %param.17), kind=kOutput, calls=%fused_computation.19 | convolution fusion | flops 1207959552 | bytes 5898240 | tf_op jit(solution)/shard_map/dot_general | solution.py:41
  333.3 39.3 %all-to-all-done.3 = bf16[64,1,6,2049]{3,2,1,0:T(8,128)(2,1)} async-done(((bf16[64,1,6,2049]{3,2,1,0:T(8,128)(2,1)}), bf16[64,1,6,2049]{3,2,1,0:T(8,128)(2,1)}, u32[]{:S(2)}, u32[]{:S(2)}) %all-to-all-start.3) | async-done | bytes 1573664 | tf_op jit(solution)/shard_map/all_to_all | solution.py:17
  377.0 3.7 convert_element_type.165
  380.8 4.8 fusion.16
  385.6 7.8 %fusion = f32[384,2048]{1,0:T(8,128)} fusion(bf16[1,1,2048,768]{3,2,1,0:T(8,128)(2,1)} %param.17, f32[384,768]{1,0:T(8,128)} %fusion.16, bf16[384,2048]{1,0:T(8,128)(2,1)} %reshape_squeeze_squeeze.7, bf16[1,1,2048,768]{3,2,1,0:T(8,128)(2,1)S(1)} %copy-done, f32[384,768]{1,0:T(8,128)} %fusion.2), kind=kOutput, calls=%fused_computation.17 | convolution fusion | flops 2418868224 | bytes 13369344 | tf_op jit(solution)/shard_map/dot_general | solution.py:35
  393.4 5.2 %add_convert_fusion = bf16[384,2048]{1,0:T(8,128)(2,1)} fusion(f32[384,2048]{1,0:T(8,128)} %fusion, bf16[1,1,2048,768]{3,2,1,0:T(8,128)(2,1)S(1)} %copy-done, f32[384,768]{1,0:T(8,128)} %fusion.16, f32[384,768]{1,0:T(8,128)} %fusion.2), kind=kOutput, calls=%fused_computation.37 | convolution fusion | flops 1211301888 | bytes 10223616 | tf_op jit(solution)/shard_map/dot_general | solution.py:35
  402.3 6.7 %all-to-all-start.4 = ((bf16[64,1,6,2048]{3,2,1,0:T(8,128)(2,1)}), bf16[64,1,6,2048]{3,2,1,0:T(8,128)(2,1)}, u32[]{:S(2)}, u32[]{:S(2)}) async-start(bf16[64,1,6,2048]{3,2,1,0:T(8,128)(2,1)} %bitcast.183), calls=%async_computation.4 | async-start | bytes 4194304 | tf_op jit(solution)/shard_map/all_to_all | solution.py:127
  411.7 44.6 %all-to-all-done.4 = bf16[64,1,6,2048]{3,2,1,0:T(8,128)(2,1)} async-done(((bf16[64,1,6,2048]{3,2,1,0:T(8,128)(2,1)}), bf16[64,1,6,2048]{3,2,1,0:T(8,128)(2,1)}, u32[]{:S(2)}, u32[]{:S(2)}) %all-to-all-start.4) | async-done | bytes 1572896 | tf_op jit(solution)/shard_map/all_to_all | solution.py:127
  460.0 4.9 %gather_fusion.1 = bf16[256,2048]{1,0:T(8,128)(2,1)} fusion(bf16[384,2048]{1,0:T(8,128)(2,1)} %reshape.340, s32[1024]{0:T(1024)S(1)} %pad_clamp_fusion), kind=kCustom, calls=%fused_computation.1.clone | custom fusion | bytes 2098176 | tf_op jit(solution)/shard_map/jit(_take)/gather | solution.py:128
  471.2 5.1 %reduce_sum.87 = f32[128,2048]{1,0:T(8,128)} reduce(f32[128,2,2048]{2,1,0:T(2,128)} %reshape.347, f32[]{:T(128)} %constant.49.clone.1), dimensions={1}, to_apply=%region_16.18 | reduce | flops 262144 | bytes 3145732 | tf_op jit(solution)/shard_map/reduce_sum | solution.py:129
  (97 shorter events, 95.1 us)
Async XLA Ops:
  0.0 188.2 %copy-start = (bf16[1,1,2048,768]{3,2,1,0:T(8,128)(2,1)S(1)}, bf16[1,1,2048,768]{3,2,1,0:T(8,128)(2,1)}, u32[]{:S(2)}) copy-start(bf16[1,1,2048,768]{3,2,1,0:T(8,128)(2,1)} %param.18) | copy-start | bytes 9437188
  9.3 3.7 copy-start.8
  19.2 16.5 %copy-start.7 = (f32[1,2048]{1,0:T(1,128)S(1)}, f32[1,2048]{1,0:T(1,128)}, u32[]{:S(2)}) copy-start(f32[1,2048]{1,0:T(1,128)} %param.16) | copy-start | bytes 24580
  19.3 65.9 %all-to-all-start = ((bf16[64,1,6,2049]{3,2,1,0:T(8,128)(2,1)}), bf16[64,1,6,2049]{3,2,1,0:T(8,128)(2,1)}, u32[]{:S(2)}, u32[]{:S(2)}) async-start(bf16[64,1,6,2049]{3,2,1,0:T(8,128)(2,1)} %maximum_bitcast_fusion), calls=%async_computation | async-start | bytes 4456448 | tf_op jit(solution)/shard_map/all_to_all | solution.py:17
  34.1 1.6 copy-start.1
  85.1 77.2 %all-to-all-start.1 = ((bf16[2,64,1,6,2048]{4,0,3,2,1:T(2,128)(2,1)}), bf16[2,64,1,6,2048]{4,0,3,2,1:T(2,128)(2,1)}, u32[]{:S(2)}, u32[]{:S(2)}) async-start(bf16[2,64,1,6,2048]{4,0,3,2,1:T(2,128)(2,1)} %copy.41), calls=%async_computation.1 | async-start | bytes 6291456 | tf_op jit(solution)/shard_map/all_to_all | solution.py:112
  204.9 56.9 %all-to-all-start.2 = ((bf16[64,1,6,2048]{3,2,1,0:T(8,128)(2,1)}), bf16[64,1,6,2048]{3,2,1,0:T(8,128)(2,1)}, u32[]{:S(2)}, u32[]{:S(2)}) async-start(bf16[64,1,6,2048]{3,2,1,0:T(8,128)(2,1)} %bitcast.184), calls=%async_computation.2 | async-start | bytes 4194304 | tf_op jit(solution)/shard_map/all_to_all | solution.py:127
  281.8 1.7 copy-start.2
  281.8 1.8 copy-start.5
  286.0 16.4 %collective-permute-start = (bf16[128,2048]{1,0:T(8,128)(2,1)}, bf16[128,2048]{1,0:T(8,128)(2,1)}, u32[]{:S(2)}, u32[]{:S(2)}) collective-permute-start(bf16[128,2048]{1,0:T(8,128)(2,1)} %fusion.58), channel_id=1, source_target_pairs={{64,0},{128,64},{192,128},{65,1},{129,65},{193,129},{66,2},{130,66... | collective-permute-start | bytes 1572872 | tf_op jit(solution)/shard_map/ppermute | solution.py:31
  318.7 53.8 %all-to-all-start.3 = ((bf16[64,1,6,2049]{3,2,1,0:T(8,128)(2,1)}), bf16[64,1,6,2049]{3,2,1,0:T(8,128)(2,1)}, u32[]{:S(2)}, u32[]{:S(2)}) async-start(bf16[64,1,6,2049]{3,2,1,0:T(8,128)(2,1)} %maximum_bitcast_fusion.1), calls=%async_computation.3 | async-start | bytes 4456448 | tf_op jit(solution)/shard_map/all_to_all | solution.py:17
  402.3 54.0 %all-to-all-start.4 = ((bf16[64,1,6,2048]{3,2,1,0:T(8,128)(2,1)}), bf16[64,1,6,2048]{3,2,1,0:T(8,128)(2,1)}, u32[]{:S(2)}, u32[]{:S(2)}) async-start(bf16[64,1,6,2048]{3,2,1,0:T(8,128)(2,1)} %bitcast.183), calls=%async_computation.4 | async-start | bytes 4194304 | tf_op jit(solution)/shard_map/all_to_all | solution.py:127
  476.3 1.7 copy-start.3
  476.3 1.8 copy-start.4
  478.0 1.8 copy-start.6
where the time goes:
time: 491 us; the launch traced here: 481 us
  waiting for transfers between devices  211 us (43%)
  local copies, waits for them, and re-layouts  121 us (25%)
  starting transfers between devices  51.8 us (11%)
  other arithmetic  51.4 us (10%)
  matrix products  45.2 us (9%)
    all_to_all x2, waiting for transfers between devices, local(): lax.all_to_all(computed, 'expert', split_axis=0, concat_axis=0, tiled=True)  91.8 us
    all_to_all x2, waiting for transfers between devices, in_one_piece(): lax.all_to_all(both, axis, split_axis=split_dim, concat_axis=concat_dim,...  56.4 us
    all_to_all x1, waiting for transfers between devices, local(): lax.all_to_all(normed_all, 'expert', split_axis=1, concat_axis=1, tiled=T...  56.2 us
    dot_general x6, matrix products, contract_last(): lax.dot_general(left, right, (((1,), (1,)), ((), ())), preferred_element_...  35.6 us
    scatter x6, local copies, waits for them, and re-layouts, place_slots(): buffer = jnp.zeros((devices_expert * EXP_DEV * slot_count,) + values.shap...  32.6 us
    all_to_all x2, starting transfers between devices, in_one_piece(): lax.all_to_all(both, axis, split_axis=split_dim, concat_axis=concat_dim,...  20.5 us
    slice x1, local copies, waits for them, and re-layouts, local(): normed_far[step_index]  17.4 us
    all_to_all x2, starting transfers between devices, local(): lax.all_to_all(computed, 'expert', split_axis=0, concat_axis=0, tiled=True)  16.4 us
  transfers between devices with their start and end apart: 6, of which 6 were waited for; matrix products, arithmetic and copies ran while one was open for 13% of the time, Pallas kernels for 0%

commit v1 on v0

v1 whole, which is shorter than its diff:
```python
import functools

import jax
import jax.numpy as jnp
from jax import lax
from jax.experimental import pallas as pl
from jax.experimental.pallas import tpu as pltpu
from jax.sharding import PartitionSpec as P

D = 2048
FFE = 768
TICKS = 2
TOK = 128
PEERS = 64
SLOTS = 6
ROWS = PEERS * SLOTS
GROUPS = 8
IN_GROUP = PEERS // GROUPS
GROUP_ROWS = IN_GROUP * SLOTS
LANES = 128
TILES = D // LANES
RELAY = 4
RELAY_ROWS = TOK // RELAY
MESH = pl.DeviceIdType.MESH


def peer(me, i, sign):
    dx, dy, dz = i // 32, (i // 8) % 4, i % 8
    x, y, z = me // 32, (me // 8) % 4, me % 8
    return ((x + dx) % 2) * 32 + ((y + sign * dy + 4) % 4) * 8 + (z + sign * dz + 8) % 8


def lanes(c):
    return slice(c * LANES, (c + 1) * LANES)


def contract_last(left, right):
    return lax.dot_general(
        left, right, (((1,), (1,)), ((), ())), preferred_element_type=jnp.float32
    )


def kernel(
    tok_ref, gate_ref, slot_ref, x_ref, entering_ref, fresh_ref, gain_ref, wg_hbm, wu_hbm, wd_hbm,
    out_ref,
    wg, wu, wd, send_a, send_b, send_c, recv_a, recv_b, recv_c,
    by_token, by_slot, rows_a, rows_b, inverse_ref, current, arrived,
    w_sem, send_sem, recv_a_sem, recv_b_sem, recv_c_sem, relay_send_sem, relay_recv_sem,
):
    me = lax.axis_index("expert")
    section = lax.axis_index("section")
    last = lax.axis_size("section") - 1

    barrier = pltpu.get_barrier_semaphore()

    def greet(i, carry):
        pl.semaphore_signal(
            barrier, inc=1, device_id=(section, peer(me, i, 1)), device_id_type=MESH
        )
        return carry

    lax.fori_loop(1, PEERS, greet, 0)

    @pl.when(section < last)
    def _():
        pl.semaphore_signal(barrier, inc=1, device_id=(section + 1, me), device_id_type=MESH)

    weight_copies = [
        pltpu.make_async_copy(src, dst, w_sem.at[n])
        for n, (src, dst) in enumerate(((wg_hbm, wg), (wu_hbm, wu), (wd_hbm, wd)))
    ]
    for copy in weight_copies:
        copy.start()

    token_tiles = by_token.reshape(TOK + 1, TILES, LANES)
    by_token[pl.ds(TOK * TILES, TILES), :] = jnp.zeros((TILES, LANES), jnp.float32)

    def load_normed(tick):
        total = jnp.zeros((TOK, LANES), jnp.float32)
        for c in range(TILES):
            x = x_ref[tick, :, lanes(c)].astype(jnp.float32)
            total = total + x * x
        inverse = lax.rsqrt(jnp.sum(total, axis=1, keepdims=True) / D + 1e-05)
        inverse_ref[tick] = jnp.broadcast_to(inverse, (TOK, LANES))
        for c in range(TILES):
            x = x_ref[tick, :, lanes(c)].astype(jnp.float32)
            by_token[pl.ds(c, TOK, stride=TILES), :] = x * inverse * gain_ref[:, lanes(c)]

    def load_current():
        for c in range(TILES):
            by_token[pl.ds(c, TOK, stride=TILES), :] = current[:, lanes(c)].astype(jnp.float32)

    def ship(src, dst, s_sem, r_sem, i, sign):
        @pl.when(i == 0)
        def _():
            pltpu.make_async_copy(src.at[pl.ds(0, SLOTS)], dst.at[pl.ds(0, SLOTS)], r_sem).start()

        @pl.when(i > 0)
        def _():
            pltpu.make_async_remote_copy(
                src_ref=src.at[pl.ds(i * SLOTS, SLOTS)],
                dst_ref=dst.at[pl.ds(i * SLOTS, SLOTS)],
                send_sem=s_sem,
                recv_sem=r_sem,
                device_id=(section, peer(me, i, sign)),
                device_id_type=MESH,
            ).start()

    def pack_normed(tick):
        def body(i, carry):
            for r in range(SLOTS):
                s = i * SLOTS + r
                send_a[tick, s] = token_tiles[tok_ref[tick, s]].astype(jnp.bfloat16)
            return carry

        lax.fori_loop(0, PEERS, body, 0)

    def ship_normed(tick):
        def body(i, carry):
            ship(send_a.at[tick], recv_a.at[tick], send_sem.at[0, tick], recv_a_sem.at[tick, i // IN_GROUP], i, 1)
            return carry

        lax.fori_loop(0, PEERS, body, 0)

    def pack_and_ship_scaled(tick):
        def body(i, carry):
            for r in range(SLOTS):
                s = i * SLOTS + r
                send_b[tick, s] = (token_tiles[tok_ref[tick, s]] * gate_ref[tick, s]).astype(jnp.bfloat16)
            ship(send_b.at[tick], recv_b.at[tick], send_sem.at[1, tick], recv_b_sem.at[tick, i // IN_GROUP], i, 1)
            return carry

        lax.fori_loop(0, PEERS, body, 0)

    def wait_bytes(ref, sem):
        pltpu.make_async_copy(ref, ref, sem).wait()

    def to_rows(tiles, rows):
        by_slot[...] = tiles.astype(jnp.float32).reshape(GROUP_ROWS * TILES, LANES)
        for c in range(TILES):
            rows[:, lanes(c)] = by_slot[pl.ds(c, GROUP_ROWS, stride=TILES), :].astype(jnp.bfloat16)

    def experts(tick):
        def body(g, carry):
            part = pl.ds(g * GROUP_ROWS, GROUP_ROWS)
            wait_bytes(recv_a.at[tick, part], recv_a_sem.at[tick, g])
            wait_bytes(recv_b.at[tick, part], recv_b_sem.at[tick, g])
            to_rows(recv_a[tick, part], rows_a)
            to_rows(recv_b[tick, part], rows_b)
            normed = rows_a[...]
            pre_gate = jnp.dot(normed, wg[...], preferred_element_type=jnp.float32)
            pre_up = jnp.dot(normed, wu[...], preferred_element_type=jnp.float32)
            hidden_grad = contract_last(rows_b[...], wd[...])
            sigmoid = jax.nn.sigmoid(pre_gate)
            gate_grad = (
                hidden_grad * pre_up * sigmoid * (1.0 + pre_gate * (1.0 - sigmoid))
            ).astype(jnp.bfloat16)
            up_grad = (hidden_grad * pre_gate * sigmoid).astype(jnp.bfloat16)
            summed = contract_last(gate_grad, wg[...]) + contract_last(up_grad, wu[...])
            for c in range(TILES):
                by_slot[pl.ds(c, GROUP_ROWS, stride=TILES), :] = summed[:, lanes(c)]
            send_c[tick, part] = by_slot[...].reshape(GROUP_ROWS, TILES, LANES).astype(jnp.bfloat16)

            def give_back(j, inner):
                ship(send_c.at[tick], recv_c.at[tick], send_sem.at[2, tick], recv_c_sem.at[tick], g * IN_GROUP + j, -1)
                return inner

            lax.fori_loop(0, IN_GROUP, give_back, 0)
            return carry

        lax.fori_loop(0, GROUPS, body, 0)

    def combine(tick):
        wait_bytes(recv_c.at[tick], recv_c_sem.at[tick])

        def add(t, carry):
            by_token[pl.ds(pl.multiple_of(t * TILES, TILES), TILES), :] = recv_c[
                tick, slot_ref[tick, 0, t]
            ].astype(jnp.float32) + recv_c[tick, slot_ref[tick, 1, t]].astype(jnp.float32)
            return carry

        lax.fori_loop(0, TOK, add, 0)
        for part in range(RELAY):
            first = part * RELAY_ROWS
            rows = slice(first, first + RELAY_ROWS)
            total = jnp.zeros((RELAY_ROWS, LANES), jnp.float32)
            for c in range(TILES):
                weighted = gain_ref[:, lanes(c)] * by_token[pl.ds(first * TILES + c, RELAY_ROWS, stride=TILES), :]
                total = total + x_ref[tick, rows, lanes(c)].astype(jnp.float32) * weighted
            project = jnp.sum(total, axis=1, keepdims=True) / D
            inverse = inverse_ref[tick, rows]
            cubed = inverse * inverse * inverse * project
            for c in range(TILES):
                weighted = gain_ref[:, lanes(c)] * by_token[pl.ds(first * TILES + c, RELAY_ROWS, stride=TILES), :]
                out_ref[tick, rows, lanes(c)] = (
                    current[rows, lanes(c)].astype(jnp.float32)
                    + inverse * weighted
                    - x_ref[tick, rows, lanes(c)].astype(jnp.float32) * cubed
                ).astype(jnp.bfloat16)
            if tick == 0:

                @pl.when(section > 0)
                def _():
                    relay(part).start()

    def relay(part):
        rows = pl.ds(part * RELAY_ROWS, RELAY_ROWS)
        return pltpu.make_async_remote_copy(
            src_ref=out_ref.at[0, rows],
            dst_ref=arrived.at[rows],
            send_sem=relay_send_sem.at[part],
            recv_sem=relay_recv_sem.at[part],
            device_id=(section - 1, me),
            device_id_type=MESH,
        )

    load_normed(0)
    pack_normed(0)
    current[...] = entering_ref[...]
    load_current()

    @pl.when(section == 0)
    def _():
        pl.semaphore_wait(barrier, PEERS - 1)

    @pl.when(section > 0)
    def _():
        pl.semaphore_wait(barrier, PEERS)

    ship_normed(0)
    pack_and_ship_scaled(0)
    load_normed(1)
    pack_normed(1)
    for copy in weight_copies:
        copy.wait()
    experts(0)
    ship_normed(1)
    combine(0)

    @pl.when(section < last)
    def _():
        for part in range(RELAY):
            rows = pl.ds(part * RELAY_ROWS, RELAY_ROWS)
            pltpu.make_async_copy(arrived.at[rows], arrived.at[rows], relay_recv_sem.at[part]).wait()
        current[...] = arrived[...]

    @pl.when(section == last)
    def _():
        current[...] = fresh_ref[...]

    load_current()
    pack_and_ship_scaled(1)
    experts(1)
    combine(1)

    @pl.when(section > 0)
    def _():
        for part in range(RELAY):
            relay(part).wait_send()

    far = pl.ds(SLOTS, ROWS - SLOTS)
    for n, sent in enumerate((send_a, send_b, send_c)):
        for tick in range(TICKS):
            wait_bytes(sent.at[tick, far], send_sem.at[n, tick])


def local(layer_input, entering, fresh, routes, gate_weights, norm_gain, w_gate, w_up, w_down):
    me = lax.axis_index("expert")
    chosen = routes[:, 0].reshape(TICKS, -1)
    order = jnp.arange(2 * TOK, dtype=jnp.int32)
    same = (chosen[:, :, None] == chosen[:, None, :]) & (order[None, :] < order[:, None])
    rank = jnp.sum(same.astype(jnp.int32), axis=2)
    dx = (chosen // 32 - me // 32) % 2
    dy = (chosen // 8 - me // 8) % 4
    dz = (chosen - me) % 8
    slot = (dx * 32 + dy * 8 + dz) * SLOTS + rank
    held = slot[:, None, :] == jnp.arange(ROWS, dtype=jnp.int32)[None, :, None]
    token = TOK + jnp.sum(jnp.where(held, order // 2 - TOK, 0), axis=2)
    gates = gate_weights[:, 0].reshape(TICKS, 1, -1).astype(jnp.float32)
    gate = jnp.sum(jnp.where(held, gates, 0.0), axis=2)
    slot = slot.reshape(TICKS, TOK, 2).transpose(0, 2, 1)

    smem = pl.BlockSpec(memory_space=pltpu.SMEM)
    vmem = pl.BlockSpec(memory_space=pltpu.VMEM)
    hbm = pl.BlockSpec(memory_space=pl.ANY)
    tiles = pltpu.VMEM((TICKS, ROWS, TILES, LANES), jnp.bfloat16)
    out = pl.pallas_call(
        kernel,
        out_shape=jax.ShapeDtypeStruct((TICKS, TOK, D), jnp.bfloat16),
        in_specs=[smem] * 3 + [vmem] * 4 + [hbm] * 3,
        out_specs=vmem,
        scratch_shapes=[
            pltpu.VMEM((D, FFE), jnp.bfloat16),
            pltpu.VMEM((D, FFE), jnp.bfloat16),
            pltpu.VMEM((FFE, D), jnp.bfloat16),
            tiles, tiles, tiles, tiles, tiles, tiles,
            pltpu.VMEM(((TOK + 1) * TILES, LANES), jnp.float32),
            pltpu.VMEM((GROUP_ROWS * TILES, LANES), jnp.float32),
            pltpu.VMEM((GROUP_ROWS, D), jnp.bfloat16),
            pltpu.VMEM((GROUP_ROWS, D), jnp.bfloat16),
            pltpu.VMEM((TICKS, TOK, LANES), jnp.float32),
            pltpu.VMEM((TOK, D), jnp.bfloat16),
            pltpu.VMEM((TOK, D), jnp.bfloat16),
            pltpu.SemaphoreType.DMA((3,)),
            pltpu.SemaphoreType.DMA((3, TICKS)),
            pltpu.SemaphoreType.DMA((TICKS, GROUPS)),
            pltpu.SemaphoreType.DMA((TICKS, GROUPS)),
            pltpu.SemaphoreType.DMA((TICKS,)),
            pltpu.SemaphoreType.DMA((RELAY,)),
            pltpu.SemaphoreType.DMA((RELAY,)),
        ],
        compiler_params=pltpu.CompilerParams(
            collective_id=0, has_side_effects=True, vmem_limit_bytes=56 << 20
        ),
    )(token, gate, slot, layer_input[:, 0], entering[0], fresh[0], norm_gain, w_gate[0, 0], w_up[0, 0], w_down[0, 0])
    return out[:, None]


def solution(mesh):
    in_specs = (
        P(None, "section", "expert", None),
        P("section", "expert", None),
        P(None, "expert", None),
        P(None, "section", "expert", None),
        P(None, "section", "expert", None),
        P("section", None),
        P("section", "expert", None, None),
        P("section", "expert", None, None),
        P("section", "expert", None, None),
    )
    out_specs = P(None, "section", "expert", None)
    return jax.shard_map(local, mesh=mesh, in_specs=in_specs, out_specs=out_specs, check_vma=False)
```

time: 491 us -> 231 us (0.47); the launches traced: 481 us -> 229 us
  Pallas kernels: 0 us -> 221 us
  waiting for transfers between devices: 211 us -> 0 us
  local copies, waits for them, and re-layouts: 121 us -> 4.41 us
  starting transfers between devices: 51.8 us -> 0 us
  other arithmetic: 51.4 us -> 3.17 us
  matrix products: 45.2 us -> 0 us
    pallas_call x0 -> x1, Pallas kernels: none -> 221 us  [local(): pl.pallas_call(kernel, out_shape=jax.ShapeDtypeStruct((TICKS, TOK, D), jn...]
    all_to_all x5 -> x0, waiting for transfers between devices: 204 us -> none  [the longest x2 91.8 us: local(): lax.all_to_all(computed, 'expert', split_axis=0, concat_axis=0, tiled=True)]
    dot_general x8 -> x0, matrix products: 45.2 us -> none  [the longest x6 35.6 us: contract_last(): lax.dot_general(left, right, (((1,), (1,)), ((), ())), preferred_element_...]
    all_to_all x5 -> x0, starting transfers between devices: 44.8 us -> none  [the longest x2 20.5 us: in_one_piece(): lax.all_to_all(both, axis, split_axis=split_dim, concat_axis=concat_dim,...]
    scatter x6 -> x0, local copies, waits for them, and re-layouts: 32.6 us -> none  [place_slots(): buffer = jnp.zeros((devices_expert * EXP_DEV * slot_count,) + values.shap...]
    another operation x14 -> x1, local copies, waits for them, and re-layouts: 28.1 us -> 0.14 us  [local(): chosen = routes[:, 0].reshape(TICKS, -1)]
    slice x9 -> x0, local copies, waits for them, and re-layouts: 19.9 us -> none  [the longest x1 17.4 us: local(): normed_far[step_index]]
    convert_element_type x11 -> x0, other arithmetic: 18.7 us -> none  [the longest x2 6.69 us: expert_side(): (gate_rows.astype(jnp.float32)[:, None] * grad_rows.astype(jnp.float32))....]
  transfers between devices with their start and end apart: 6 -> 0, of which waited for: 6 -> 0; matrix products, arithmetic and copies ran while one was open for 13% -> 0% of each run, Pallas kernels for 0% -> 0%
where the time goes in v1:
time: 231 us; the launch traced here: 229 us
  Pallas kernels  221 us (96%)
  local copies, waits for them, and re-layouts  4.41 us (2%)
  other arithmetic  3.17 us (1%)
    pallas_call x1, Pallas kernels, local(): pl.pallas_call(kernel, out_shape=jax.ShapeDtypeStruct((TICKS, TOK, D), jn...  221 us

profile of v1, /device:TPU:1, one launch (start us, length us, event | category | flops | bytes accessed | tf_op | source)
XLA Modules:
  0.0 228.9 jit_solution(15795084261724432109)
XLA Ops:
  0.0 0.8 copy.16
  0.8 0.1 reshape.111
  1.0 0.8 copy.15
  1.8 0.1 reshape_squeeze.6
  1.9 0.3 convert_reduce_fusion
  2.2 0.8 select_reduce_fusion.gate_ref
  3.0 0.2 select_reduce_fusion.1
  3.2 0.6 broadcast_add_fusion.tok_ref
  3.8 0.1 reduce_sum.32
  3.9 0.1 copy.17
  4.0 1.3 add_bitcast_fusion.slot_ref
  5.3 221.3 %shard_map.91 = bf16[2,128,2048]{2,1,0:T(8,128)(2,1)} custom-call(s32[2,384]{1,0:T(2,128)} %broadcast_add_fusion.tok_ref, f32[2,384]{1,0:T(2,128)} %select_reduce_fusion.gate_ref, s32[2,2,128]{2,1,0:T(2,128)} %add_bitcast_fusion.slot_ref, bf16[2,128,2048]{2,1,0:T(8,128)(2,1)} %bitcast.42, bf16[128,2048]{1,0:T(8,128)(2,1)} %bitcast.43, ...), custom_call_target="tpu_custom_call" | custom-call | tf_op jit(solution)/shard_map/pallas_call | solution.py:287
  226.6 2.3 %copy.20 = bf16[2,1,128,2048]{3,2,1,0:T(8,128)(2,1)} copy(bf16[2,1,128,2048]{3,2,1,0:T(8,128)(2,1)} %bitcast.38) | data formatting | bytes 2097152
  (3 shorter events, 0.1 us)

commit v2 on v1

--- a/solution.py
+++ b/solution.py
@@ -21,7 +21,11 @@
 TILES = D // LANES
 RELAY = 4
 RELAY_ROWS = TOK // RELAY
+UNROLL = 8
 MESH = pl.DeviceIdType.MESH
+
+OWN, BEHIND, AHEAD = range(3)
+SHIFT = (0, 1, -1)
 
 
 def peer(me, i, sign):
@@ -43,9 +47,10 @@
 def kernel(
     tok_ref, gate_ref, slot_ref, x_ref, entering_ref, fresh_ref, gain_ref, wg_hbm, wu_hbm, wd_hbm,
     out_ref,
-    wg, wu, wd, send_a, send_b, send_c, recv_a, recv_b, recv_c,
+    wg, wu, wd, send_a, send_b, send_c, recv_a, recv_b, recv_c, blocks_a, blocks_b, toks, gates,
     by_token, by_slot, rows_a, rows_b, inverse_ref, current, arrived,
     w_sem, send_sem, recv_a_sem, recv_b_sem, recv_c_sem, relay_send_sem, relay_recv_sem,
+    block_send_sem, block_recv_sem, table_send_sem, table_recv_sem,
 ):
     me = lax.axis_index("expert")
     section = lax.axis_index("section")
@@ -72,8 +77,16 @@
     for copy in weight_copies:
         copy.start()
 
-    token_tiles = by_token.reshape(TOK + 1, TILES, LANES)
-    by_token[pl.ds(TOK * TILES, TILES), :] = jnp.zeros((TILES, LANES), jnp.float32)
+    toks = (tok_ref, *toks)
+    gates = (gate_ref, *gates)
+    for tick_blocks in (*blocks_a, *blocks_b):
+        for block in tick_blocks:
+            block[TOK] = jnp.zeros((TILES, LANES), jnp.bfloat16)
+
+    def store_block(block):
+        for part in range(RELAY):
+            rows = by_token[pl.ds(part * RELAY_ROWS * TILES, RELAY_ROWS * TILES), :]
+            block[pl.ds(part * RELAY_ROWS, RELAY_ROWS)] = rows.reshape(RELAY_ROWS, TILES, LANES).astype(jnp.bfloat16)
 
     def load_normed(tick):
         total = jnp.zeros((TOK, LANES), jnp.float32)
@@ -85,52 +98,101 @@
         for c in range(TILES):
             x = x_ref[tick, :, lanes(c)].astype(jnp.float32)
             by_token[pl.ds(c, TOK, stride=TILES), :] = x * inverse * gain_ref[:, lanes(c)]
-
-    def load_current():
+        store_block(blocks_a[tick][OWN])
+
+    def load_current(tick):
         for c in range(TILES):
             by_token[pl.ds(c, TOK, stride=TILES), :] = current[:, lanes(c)].astype(jnp.float32)
-
-    def ship(src, dst, s_sem, r_sem, i, sign):
-        @pl.when(i == 0)
+        store_block(blocks_b[tick][OWN])
+
+    def along_z(src, dst, s_sem, r_sem, step):
+        return pltpu.make_async_remote_copy(
+            src_ref=src, dst_ref=dst, send_sem=s_sem, recv_sem=r_sem,
+            device_id=(section, peer(me, 1, step)), device_id_type=MESH,
+        )
+
+    def block_copies(kind, tick):
+        blocks = (blocks_a, blocks_b)[kind][tick]
+        whole = pl.ds(0, TOK)
+        return [
+            along_z(
+                blocks[OWN].at[whole], blocks[side].at[whole],
+                block_send_sem.at[kind, tick, side - 1], block_recv_sem.at[kind, tick, side - 1], SHIFT[side],
+            )
+            for side in (BEHIND, AHEAD)
+        ]
+
+    table_copies = [
+        along_z(
+            table[OWN], table[side],
+            table_send_sem.at[n, side - 1], table_recv_sem.at[n, side - 1], SHIFT[side],
+        )
+        for n, table in enumerate((toks, gates))
+        for side in (BEHIND, AHEAD)
+    ]
+
+    def start(copies):
+        for copy in copies:
+            copy.start()
+
+    def await_arrival(copies):
+        for copy in copies:
+            copy.wait_recv()
+
+    def stay(src, dst, r_sem, i):
+        part = pl.ds(i * SLOTS, SLOTS)
+        pltpu.make_async_copy(src.at[part], dst.at[part], r_sem).start()
+
+    def send(src, dst, s_sem, r_sem, i, device):
+        part = pl.ds(i * SLOTS, SLOTS)
+        pltpu.make_async_remote_copy(
+            src_ref=src.at[part], dst_ref=dst.at[part], send_sem=s_sem, recv_sem=r_sem,
+            device_id=(section, device), device_id_type=MESH,
+        ).start()
+
+    def pack(kind, tick, side, q, dz):
+        i = q * 8 + dz
+        for r in range(SLOTS):
+            s = i * SLOTS + r
+            if kind == 0:
+                send_a[tick, s] = blocks_a[tick][side][toks[side][tick, s]]
+            else:
+                rows = blocks_b[tick][side][toks[side][tick, s]].astype(jnp.float32)
+                send_b[tick, s] = (rows * gates[side][tick, s]).astype(jnp.bfloat16)
+        src, dst = ((send_a, recv_a), (send_b, recv_b))[kind]
+        src, dst, s_sem = src.at[tick], dst.at[tick], send_sem.at[kind, tick]
+        r_sem = (recv_a_sem, recv_b_sem)[kind].at[tick, q]
+        left = (dz - SHIFT[side]) % 8
+        if left != 0:
+            send(src, dst, s_sem, r_sem, i, peer(me, q * 8 + left, 1))
+            return
+
+        @pl.when(q == 0)
         def _():
-            pltpu.make_async_copy(src.at[pl.ds(0, SLOTS)], dst.at[pl.ds(0, SLOTS)], r_sem).start()
-
-        @pl.when(i > 0)
+            stay(src, dst, r_sem, i)
+
+        @pl.when(q > 0)
         def _():
-            pltpu.make_async_remote_copy(
-                src_ref=src.at[pl.ds(i * SLOTS, SLOTS)],
-                dst_ref=dst.at[pl.ds(i * SLOTS, SLOTS)],
-                send_sem=s_sem,
-                recv_sem=r_sem,
-                device_id=(section, peer(me, i, sign)),
-                device_id_type=MESH,
-            ).start()
-
-    def pack_normed(tick):
-        def body(i, carry):
-            for r in range(SLOTS):
-                s = i * SLOTS + r
-                send_a[tick, s] = token_tiles[tok_ref[tick, s]].astype(jnp.bfloat16)
+            send(src, dst, s_sem, r_sem, i, peer(me, q * 8, 1))
+
+    def pack_own(kind, tick):
+        def body(q, carry):
+            pack(kind, tick, OWN, q, 0)
             return carry
 
-        lax.fori_loop(0, PEERS, body, 0)
-
-    def ship_normed(tick):
-        def body(i, carry):
-            ship(send_a.at[tick], recv_a.at[tick], send_sem.at[0, tick], recv_a_sem.at[tick, i // IN_GROUP], i, 1)
+        lax.fori_loop(0, GROUPS, body, 0)
+
+    def pack_sides(kind, tick):
+        def body(half, carry):
+            for odd in range(2):
+                q = half * 2 + odd
+                for dz in range(1, 4):
+                    pack(kind, tick, BEHIND, q, dz)
+                    pack(kind, tick, AHEAD, q, 8 - dz)
+                pack(kind, tick, (BEHIND, AHEAD)[odd], q, 4)
             return carry
 
-        lax.fori_loop(0, PEERS, body, 0)
-
-    def pack_and_ship_scaled(tick):
-        def body(i, carry):
-            for r in range(SLOTS):
-                s = i * SLOTS + r
-                send_b[tick, s] = (token_tiles[tok_ref[tick, s]] * gate_ref[tick, s]).astype(jnp.bfloat16)
-            ship(send_b.at[tick], recv_b.at[tick], send_sem.at[1, tick], recv_b_sem.at[tick, i // IN_GROUP], i, 1)
-            return carry
-
-        lax.fori_loop(0, PEERS, body, 0)
+        lax.fori_loop(0, GROUPS // 2, body, 0)
 
     def wait_bytes(ref, sem):
         pltpu.make_async_copy(ref, ref, sem).wait()
@@ -162,7 +224,19 @@
             send_c[tick, part] = by_slot[...].reshape(GROUP_ROWS, TILES, LANES).astype(jnp.bfloat16)
 
             def give_back(j, inner):
-                ship(send_c.at[tick], recv_c.at[tick], send_sem.at[2, tick], recv_c_sem.at[tick], g * IN_GROUP + j, -1)
+                i = g * IN_GROUP + j
+
+                @pl.when(i == 0)
+                def _():
+                    stay(send_c.at[tick], recv_c.at[tick], recv_c_sem.at[tick], i)
+
+                @pl.when(i > 0)
+                def _():
+                    send(
+                        send_c.at[tick], recv_c.at[tick], send_sem.at[2, tick], recv_c_sem.at[tick],
+                        i, peer(me, i, -1),
+                    )
+
                 return inner
 
             lax.fori_loop(0, IN_GROUP, give_back, 0)
@@ -173,13 +247,15 @@
     def combine(tick):
         wait_bytes(recv_c.at[tick], recv_c_sem.at[tick])
 
-        def add(t, carry):
-            by_token[pl.ds(pl.multiple_of(t * TILES, TILES), TILES), :] = recv_c[
-                tick, slot_ref[tick, 0, t]
-            ].astype(jnp.float32) + recv_c[tick, slot_ref[tick, 1, t]].astype(jnp.float32)
+        def add(n, carry):
+            for u in range(UNROLL):
+                t = n * UNROLL + u
+                by_token[pl.ds(pl.multiple_of(t * TILES, TILES), TILES), :] = recv_c[
+                    tick, slot_ref[tick, 0, t]
+                ].astype(jnp.float32) + recv_c[tick, slot_ref[tick, 1, t]].astype(jnp.float32)
             return carry
 
-        lax.fori_loop(0, TOK, add, 0)
+        lax.fori_loop(0, TOK // UNROLL, add, 0)
         for part in range(RELAY):
             first = part * RELAY_ROWS
             rows = slice(first, first + RELAY_ROWS)
@@ -214,42 +290,54 @@
             device_id_type=MESH,
         )
 
+    current[...] = entering_ref[...]
+    load_current(0)
+
+    @pl.when(section == 0)
+    def _():
+        pl.semaphore_wait(barrier, PEERS - 1)
+
+    @pl.when(section > 0)
+    def _():
+        pl.semaphore_wait(barrier, PEERS)
+
+    start(table_copies)
+    start(block_copies(1, 0))
     load_normed(0)
-    pack_normed(0)
-    current[...] = entering_ref[...]
-    load_current()
-
-    @pl.when(section == 0)
-    def _():
-        pl.semaphore_wait(barrier, PEERS - 1)
-
-    @pl.when(section > 0)
-    def _():
-        pl.semaphore_wait(barrier, PEERS)
-
-    ship_normed(0)
-    pack_and_ship_scaled(0)
+    start(block_copies(0, 0))
+    pack_own(1, 0)
+    pack_own(0, 0)
     load_normed(1)
-    pack_normed(1)
+    await_arrival(table_copies)
+    await_arrival(block_copies(1, 0))
+    pack_sides(1, 0)
+    await_arrival(block_copies(0, 0))
+    pack_sides(0, 0)
     for copy in weight_copies:
         copy.wait()
     experts(0)
-    ship_normed(1)
+    start(block_copies(0, 1))
+    pack_own(0, 1)
     combine(0)
 
     @pl.when(section < last)
     def _():
         for part in range(RELAY):
             rows = pl.ds(part * RELAY_ROWS, RELAY_ROWS)
-            pltpu.make_async_copy(arrived.at[rows], arrived.at[rows], relay_recv_sem.at[part]).wait()
+            wait_bytes(arrived.at[rows], relay_recv_sem.at[part])
         current[...] = arrived[...]
 
     @pl.when(section == last)
     def _():
         current[...] = fresh_ref[...]
 
-    load_current()
-    pack_and_ship_scaled(1)
+    load_current(1)
+    start(block_copies(1, 1))
+    pack_own(1, 1)
+    await_arrival(block_copies(0, 1))
+    pack_sides(0, 1)
+    await_arrival(block_copies(1, 1))
+    pack_sides(1, 1)
     experts(1)
     combine(1)
 
@@ -258,10 +346,15 @@
         for part in range(RELAY):
             relay(part).wait_send()
 
-    far = pl.ds(SLOTS, ROWS - SLOTS)
-    for n, sent in enumerate((send_a, send_b, send_c)):
+    for copy in table_copies:
+        copy.wait_send()
+    for kind in range(2):
         for tick in range(TICKS):
-            wait_bytes(sent.at[tick, far], send_sem.at[n, tick])
+            for copy in block_copies(kind, tick):
+                copy.wait_send()
+    for kind, (sent, stayed) in enumerate(((send_a, 3), (send_b, 3), (send_c, 1))):
+        for tick in range(TICKS):
+            wait_bytes(sent.at[tick, pl.ds(stayed * SLOTS, ROWS - stayed * SLOTS)], send_sem.at[kind, tick])
 
 
 def local(layer_input, entering, fresh, routes, gate_weights, norm_gain, w_gate, w_up, w_down):
@@ -284,6 +377,7 @@
     vmem = pl.BlockSpec(memory_space=pltpu.VMEM)
     hbm = pl.BlockSpec(memory_space=pl.ANY)
     tiles = pltpu.VMEM((TICKS, ROWS, TILES, LANES), jnp.bfloat16)
+    blocks = [[pltpu.VMEM((TOK + 1, TILES, LANES), jnp.bfloat16)] * 3] * TICKS
     out = pl.pallas_call(
         kernel,
         out_shape=jax.ShapeDtypeStruct((TICKS, TOK, D), jnp.bfloat16),
@@ -294,7 +388,10 @@
             pltpu.VMEM((D, FFE), jnp.bfloat16),
             pltpu.VMEM((FFE, D), jnp.bfloat16),
             tiles, tiles, tiles, tiles, tiles, tiles,
-            pltpu.VMEM(((TOK + 1) * TILES, LANES), jnp.float32),
+            blocks, blocks,
+            [pltpu.SMEM((TICKS, ROWS), jnp.int32)] * 2,
+            [pltpu.SMEM((TICKS, ROWS), jnp.float32)] * 2,
+            pltpu.VMEM((TOK * TILES, LANES), jnp.float32),
             pltpu.VMEM((GROUP_ROWS * TILES, LANES), jnp.float32),
             pltpu.VMEM((GROUP_ROWS, D), jnp.bfloat16),
             pltpu.VMEM((GROUP_ROWS, D), jnp.bfloat16),
@@ -308,6 +405,10 @@
             pltpu.SemaphoreType.DMA((TICKS,)),
             pltpu.SemaphoreType.DMA((RELAY,)),
             pltpu.SemaphoreType.DMA((RELAY,)),
+            pltpu.SemaphoreType.DMA((2, TICKS, 2)),
+            pltpu.SemaphoreType.DMA((2, TICKS, 2)),
+            pltpu.SemaphoreType.DMA((2, 2)),
+            pltpu.SemaphoreType.DMA((2, 2)),
         ],
         compiler_params=pltpu.CompilerParams(
             collective_id=0, has_side_effects=True, vmem_limit_bytes=56 << 20

time: 231 us -> 221 us (0.957)
  Pallas kernels: 221 us -> 213 us
    pallas_call x1, Pallas kernels: 221 us -> 213 us  [local(): pl.pallas_call(kernel, out_shape=jax.ShapeDtypeStruct((TICKS, TOK, D), jn...]
where the time goes in v2:
time: 221 us; the launch traced here: 220 us
  Pallas kernels  213 us (96%)
  local copies, waits for them, and re-layouts  4.41 us (2%)
  other arithmetic  3.17 us (1%)
    pallas_call x1, Pallas kernels, local(): pl.pallas_call(kernel, out_shape=jax.ShapeDtypeStruct((TICKS, TOK, D), jn...  213 us

profile of v2, /device:TPU:1, one launch (start us, length us, event | category | flops | bytes accessed | tf_op | source)
XLA Modules:
  0.0 220.4 jit_solution(10399328545854400543)
XLA Ops:
  0.0 0.8 copy.16
  0.8 0.1 reshape.111
  1.0 0.8 copy.15
  1.8 0.1 reshape_squeeze.6
  1.9 0.3 convert_reduce_fusion
  2.2 0.8 select_reduce_fusion.gate_ref
  3.0 0.2 select_reduce_fusion.1
  3.2 0.6 broadcast_add_fusion.tok_ref
  3.8 0.1 reduce_sum.32
  3.9 0.1 copy.17
  4.0 1.3 add_bitcast_fusion.slot_ref
  5.3 212.8 %shard_map.91 = bf16[2,128,2048]{2,1,0:T(8,128)(2,1)} custom-call(s32[2,384]{1,0:T(2,128)} %broadcast_add_fusion.tok_ref, f32[2,384]{1,0:T(2,128)} %select_reduce_fusion.gate_ref, s32[2,2,128]{2,1,0:T(2,128)} %add_bitcast_fusion.slot_ref, bf16[2,128,2048]{2,1,0:T(8,128)(2,1)} %bitcast.42, bf16[128,2048]{1,0:T(8,128)(2,1)} %bitcast.43, ...), custom_call_target="tpu_custom_call" | custom-call | tf_op jit(solution)/shard_map/pallas_call | solution.py:381
  218.1 2.3 %copy.20 = bf16[2,1,128,2048]{3,2,1,0:T(8,128)(2,1)} copy(bf16[2,1,128,2048]{3,2,1,0:T(8,128)(2,1)} %bitcast.38) | data formatting | bytes 2097152
  (3 shorter events, 0.1 us)

commit v3 on v2

--- a/solution.py
+++ b/solution.py
@@ -45,12 +45,13 @@
 
 
 def kernel(
-    tok_ref, gate_ref, slot_ref, x_ref, entering_ref, fresh_ref, gain_ref, wg_hbm, wu_hbm, wd_hbm,
+    routes_ref, gates_ref, x_ref, entering_ref, fresh_ref, gain_ref, wg_hbm, wu_hbm, wd_hbm,
     out_ref,
-    wg, wu, wd, send_a, send_b, send_c, recv_a, recv_b, recv_c, blocks_a, blocks_b, toks, gates,
+    wg, wu, wd, send_a, send_b, send_c, recv_a, recv_b, recv_c, blocks_a, blocks_b, toks, gates, slot_ref,
+    tok_made, gate_made, slot_made,
     by_token, by_slot, rows_a, rows_b, inverse_ref, current, arrived,
     w_sem, send_sem, recv_a_sem, recv_b_sem, recv_c_sem, relay_send_sem, relay_recv_sem,
-    block_send_sem, block_recv_sem, table_send_sem, table_recv_sem,
+    block_send_sem, block_recv_sem, table_send_sem, table_recv_sem, made_sem, greet_sem,
 ):
     me = lax.axis_index("expert")
     section = lax.axis_index("section")
@@ -58,13 +59,12 @@
 
     barrier = pltpu.get_barrier_semaphore()
 
-    def greet(i, carry):
-        pl.semaphore_signal(
-            barrier, inc=1, device_id=(section, peer(me, i, 1)), device_id_type=MESH
-        )
-        return carry
-
-    lax.fori_loop(1, PEERS, greet, 0)
+    def greet(sem, i):
+        pl.semaphore_signal(sem, inc=1, device_id=(section, peer(me, i, 1)), device_id_type=MESH)
+
+    ring_z, ring_y, ring_x = range(1, 8), (8, 16, 24), (32,)
+    for i in (*ring_z, *ring_y, *ring_x):
+        greet(barrier, i)
 
     @pl.when(section < last)
     def _():
@@ -77,8 +77,6 @@
     for copy in weight_copies:
         copy.start()
 
-    toks = (tok_ref, *toks)
-    gates = (gate_ref, *gates)
     for tick_blocks in (*blocks_a, *blocks_b):
         for block in tick_blocks:
             block[TOK] = jnp.zeros((TILES, LANES), jnp.bfloat16)
@@ -182,7 +180,7 @@
 
         lax.fori_loop(0, GROUPS, body, 0)
 
-    def pack_sides(kind, tick):
+    def pack_sides(kind, tick, first=0, end=GROUPS // 2):
         def body(half, carry):
             for odd in range(2):
                 q = half * 2 + odd
@@ -192,7 +190,7 @@
                 pack(kind, tick, (BEHIND, AHEAD)[odd], q, 4)
             return carry
 
-        lax.fori_loop(0, GROUPS // 2, body, 0)
+        lax.fori_loop(first, end, body, 0)
 
     def wait_bytes(ref, sem):
         pltpu.make_async_copy(ref, ref, sem).wait()
@@ -290,24 +288,71 @@
             device_id_type=MESH,
         )
 
+    def make_tables():
+        down = lax.broadcasted_iota(jnp.int32, (TOK, TOK), 0)
+        across = lax.broadcasted_iota(jnp.int32, (TOK, TOK), 1)
+        slot_at = lax.broadcasted_iota(jnp.int32, (TOK, ROWS), 1)
+        token_less = lax.broadcasted_iota(jnp.int32, (TOK, ROWS), 0) - TOK
+
+        def column(row):
+            return jnp.sum(jnp.where(down == across, row, jnp.zeros_like(row)), axis=1, keepdims=True)
+
+        x, y, z = me // 32, (me // 8) % 4, me % 8
+        for tick in range(TICKS):
+            chosen = [routes_ref[tick, k : k + 1, :] for k in range(2)]
+            columns = [column(row) for row in chosen]
+            token = jnp.zeros((1, ROWS), jnp.int32)
+            gate = jnp.zeros((1, ROWS), jnp.float32)
+            for k in range(2):
+                rank = jnp.zeros((1, TOK), jnp.int32)
+                for other in columns:
+                    same = (other == chosen[k]) & (down < across)
+                    rank = rank + jnp.sum(jnp.where(same, 1, 0), axis=0, keepdims=True)
+                dx = ((chosen[k] >> 5) - x) & 1
+                dy = ((chosen[k] >> 3) - y) & 3
+                dz = (chosen[k] - z) & 7
+                slot = ((dx << 5) + (dy << 3) + dz) * SLOTS + rank
+                slot_made[tick, k : k + 1, :] = jnp.minimum(slot, ROWS - 1)
+                held = column(slot) == slot_at
+                gate_column = column(gates_ref[tick, k : k + 1, :].astype(jnp.float32))
+                token = token + jnp.sum(jnp.where(held, token_less, 0), axis=0, keepdims=True)
+                gate = gate + jnp.sum(jnp.where(held, gate_column, 0.0), axis=0, keepdims=True)
+            tok_made[tick : tick + 1, :] = jnp.clip(token + TOK, 0, TOK)
+            gate_made[tick : tick + 1, :] = gate
+
     current[...] = entering_ref[...]
     load_current(0)
 
     @pl.when(section == 0)
     def _():
-        pl.semaphore_wait(barrier, PEERS - 1)
+        pl.semaphore_wait(barrier, 11)
 
     @pl.when(section > 0)
     def _():
-        pl.semaphore_wait(barrier, PEERS)
-
-    start(table_copies)
+        pl.semaphore_wait(barrier, 12)
+
+    for i in ring_y:
+        greet(greet_sem.at[0], i)
     start(block_copies(1, 0))
     load_normed(0)
     start(block_copies(0, 0))
+    make_tables()
+    made_copies = [
+        pltpu.make_async_copy(made, held, made_sem.at[n])
+        for n, (made, held) in enumerate(((tok_made, toks[OWN]), (gate_made, gates[OWN]), (slot_made, slot_ref)))
+    ]
+    start(made_copies)
+    pl.semaphore_wait(greet_sem.at[0], 3)
+    for i in ring_x:
+        greet(greet_sem.at[1], i)
+    for copy in made_copies:
+        copy.wait()
+    start(table_copies)
+    load_normed(1)
+    start(block_copies(0, 1))
+    pl.semaphore_wait(greet_sem.at[1], 1)
     pack_own(1, 0)
     pack_own(0, 0)
-    load_normed(1)
     await_arrival(table_copies)
     await_arrival(block_copies(1, 0))
     pack_sides(1, 0)
@@ -316,8 +361,9 @@
     for copy in weight_copies:
         copy.wait()
     experts(0)
-    start(block_copies(0, 1))
     pack_own(0, 1)
+    await_arrival(block_copies(0, 1))
+    pack_sides(0, 1, 0, 2)
     combine(0)
 
     @pl.when(section < last)
@@ -334,8 +380,7 @@
     load_current(1)
     start(block_copies(1, 1))
     pack_own(1, 1)
-    await_arrival(block_copies(0, 1))
-    pack_sides(0, 1)
+    pack_sides(0, 1, 2, 4)
     await_arrival(block_copies(1, 1))
     pack_sides(1, 1)
     experts(1)
@@ -358,22 +403,7 @@
 
 
 def local(layer_input, entering, fresh, routes, gate_weights, norm_gain, w_gate, w_up, w_down):
-    me = lax.axis_index("expert")
-    chosen = routes[:, 0].reshape(TICKS, -1)
-    order = jnp.arange(2 * TOK, dtype=jnp.int32)
-    same = (chosen[:, :, None] == chosen[:, None, :]) & (order[None, :] < order[:, None])
-    rank = jnp.sum(same.astype(jnp.int32), axis=2)
-    dx = (chosen // 32 - me // 32) % 2
-    dy = (chosen // 8 - me // 8) % 4
-    dz = (chosen - me) % 8
-    slot = (dx * 32 + dy * 8 + dz) * SLOTS + rank
-    held = slot[:, None, :] == jnp.arange(ROWS, dtype=jnp.int32)[None, :, None]
-    token = TOK + jnp.sum(jnp.where(held, order // 2 - TOK, 0), axis=2)
-    gates = gate_weights[:, 0].reshape(TICKS, 1, -1).astype(jnp.float32)
-    gate = jnp.sum(jnp.where(held, gates, 0.0), axis=2)
-    slot = slot.reshape(TICKS, TOK, 2).transpose(0, 2, 1)
-
-    smem = pl.BlockSpec(memory_space=pltpu.SMEM)
+    by_choice = [a[:, 0].transpose(0, 2, 1) for a in (routes, gate_weights)]
     vmem = pl.BlockSpec(memory_space=pltpu.VMEM)
     hbm = pl.BlockSpec(memory_space=pl.ANY)
     tiles = pltpu.VMEM((TICKS, ROWS, TILES, LANES), jnp.bfloat16)
@@ -381,7 +411,7 @@
     out = pl.pallas_call(
         kernel,
         out_shape=jax.ShapeDtypeStruct((TICKS, TOK, D), jnp.bfloat16),
-        in_specs=[smem] * 3 + [vmem] * 4 + [hbm] * 3,
+        in_specs=[vmem] * 6 + [hbm] * 3,
         out_specs=vmem,
         scratch_shapes=[
             pltpu.VMEM((D, FFE), jnp.bfloat16),
@@ -389,8 +419,12 @@
             pltpu.VMEM((FFE, D), jnp.bfloat16),
             tiles, tiles, tiles, tiles, tiles, tiles,
             blocks, blocks,
-            [pltpu.SMEM((TICKS, ROWS), jnp.int32)] * 2,
-            [pltpu.SMEM((TICKS, ROWS), jnp.float32)] * 2,
+            [pltpu.SMEM((TICKS, ROWS), jnp.int32)] * 3,
+            [pltpu.SMEM((TICKS, ROWS), jnp.float32)] * 3,
+            pltpu.SMEM((TICKS, 2, TOK), jnp.int32),
+            pltpu.VMEM((TICKS, ROWS), jnp.int32),
+            pltpu.VMEM((TICKS, ROWS), jnp.float32),
+            pltpu.VMEM((TICKS, 2, TOK), jnp.int32),
             pltpu.VMEM((TOK * TILES, LANES), jnp.float32),
             pltpu.VMEM((GROUP_ROWS * TILES, LANES), jnp.float32),
             pltpu.VMEM((GROUP_ROWS, D), jnp.bfloat16),
@@ -409,11 +443,13 @@
             pltpu.SemaphoreType.DMA((2, TICKS, 2)),
             pltpu.SemaphoreType.DMA((2, 2)),
             pltpu.SemaphoreType.DMA((2, 2)),
+            pltpu.SemaphoreType.DMA((3,)),
+            pltpu.SemaphoreType.REGULAR((2,)),
         ],
         compiler_params=pltpu.CompilerParams(
             collective_id=0, has_side_effects=True, vmem_limit_bytes=56 << 20
         ),
-    )(token, gate, slot, layer_input[:, 0], entering[0], fresh[0], norm_gain, w_gate[0, 0], w_up[0, 0], w_down[0, 0])
+    )(*by_choice, layer_input[:, 0], entering[0], fresh[0], norm_gain, w_gate[0, 0], w_up[0, 0], w_down[0, 0])
     return out[:, None]
 
 

time: 221 us -> 215 us (0.973)
  other arithmetic: 3.17 us -> 0 us
where the time goes in v3:
time: 215 us
  Pallas kernels  212 us (99%)
  local copies, waits for them, and re-layouts  2.3 us (1%)
    pallas_call x1, Pallas kernels, local(): pl.pallas_call(kernel, out_shape=jax.ShapeDtypeStruct((TICKS, TOK, D), jn...  212 us

profile of v3, /device:TPU:1, one launch (start us, length us, event | category | flops | bytes accessed | tf_op | source)
XLA Modules:
  0.0 214.6 jit_solution(14313177229208710476)
XLA Ops:
  0.0 212.3 %shard_map.91 = bf16[2,128,2048]{2,1,0:T(8,128)(2,1)} custom-call(s32[2,2,128]{2,1,0:T(2,128)} %bitcast.22, bf16[2,2,128]{2,1,0:T(2,128)(2,1)} %bitcast.23, bf16[2,128,2048]{2,1,0:T(8,128)(2,1)} %bitcast.19, bf16[128,2048]{1,0:T(8,128)(2,1)} %bitcast.20, bf16[128,2048]{1,0:T(8,128)(2,1)} %bitcast.21, f32[1,2048]{1,0:T(1,128)} %gain_ref.1, ...), custom_call_target="tpu_custom_call" | custom-call | tf_op jit(solution)/shard_map/pallas_call | solution.py:411
  212.3 2.3 %copy.12 = bf16[2,1,128,2048]{3,2,1,0:T(8,128)(2,1)} copy(bf16[2,1,128,2048]{3,2,1,0:T(8,128)(2,1)} %bitcast.15) | data formatting | bytes 2097152

commit v4 on v3

--- a/solution.py
+++ b/solution.py
@@ -56,6 +56,7 @@
     me = lax.axis_index("expert")
     section = lax.axis_index("section")
     last = lax.axis_size("section") - 1
+    lower = section < 2
 
     barrier = pltpu.get_barrier_semaphore()
 
@@ -366,6 +367,10 @@
     pack_sides(0, 1, 0, 2)
     combine(0)
 
+    @pl.when(lower)
+    def _():
+        pack_sides(0, 1, 2, 4)
+
     @pl.when(section < last)
     def _():
         for part in range(RELAY):
@@ -380,7 +385,11 @@
     load_current(1)
     start(block_copies(1, 1))
     pack_own(1, 1)
-    pack_sides(0, 1, 2, 4)
+
+    @pl.when(~lower)
+    def _():
+        pack_sides(0, 1, 2, 4)
+
     await_arrival(block_copies(1, 1))
     pack_sides(1, 1)
     experts(1)

time: 215 us -> 210 us (0.977)
  Pallas kernels: 212 us -> 207 us
    pallas_call x1, Pallas kernels: 212 us -> 207 us  [local(): pl.pallas_call(kernel, out_shape=jax.ShapeDtypeStruct((TICKS, TOK, D), jn...]
where the time goes in v4:
time: 210 us; the launch traced here: 209 us
  Pallas kernels  207 us (99%)
  local copies, waits for them, and re-layouts  2.3 us (1%)
    pallas_call x1, Pallas kernels, local(): pl.pallas_call(kernel, out_shape=jax.ShapeDtypeStruct((TICKS, TOK, D), jn...  207 us

profile of v4, /device:TPU:1, one launch (start us, length us, event | category | flops | bytes accessed | tf_op | source)
XLA Modules:
  0.0 209.1 jit_solution(5089570159134682024)
XLA Ops:
  0.0 206.8 %shard_map.91 = bf16[2,128,2048]{2,1,0:T(8,128)(2,1)} custom-call(s32[2,2,128]{2,1,0:T(2,128)} %bitcast.22, bf16[2,2,128]{2,1,0:T(2,128)(2,1)} %bitcast.23, bf16[2,128,2048]{2,1,0:T(8,128)(2,1)} %bitcast.19, bf16[128,2048]{1,0:T(8,128)(2,1)} %bitcast.20, bf16[128,2048]{1,0:T(8,128)(2,1)} %bitcast.21, f32[1,2048]{1,0:T(1,128)} %gain_ref.1, ...), custom_call_target="tpu_custom_call" | custom-call | tf_op jit(solution)/shard_map/pallas_call | solution.py:420
  206.8 2.3 %copy.12 = bf16[2,1,128,2048]{3,2,1,0:T(8,128)(2,1)} copy(bf16[2,1,128,2048]{3,2,1,0:T(8,128)(2,1)} %bitcast.15) | data formatting | bytes 2097152

commit v5 on v4

--- a/solution.py
+++ b/solution.py
@@ -22,6 +22,7 @@
 RELAY = 4
 RELAY_ROWS = TOK // RELAY
 UNROLL = 8
+PART_ROWS = 16
 MESH = pl.DeviceIdType.MESH
 
 OWN, BEHIND, AHEAD = range(3)
@@ -45,12 +46,12 @@
 
 
 def kernel(
-    routes_ref, gates_ref, x_ref, entering_ref, fresh_ref, gain_ref, wg_hbm, wu_hbm, wd_hbm,
+    routes_ref, gates_ref, entering_ref, gain_ref, x_hbm, fresh_hbm, wg_hbm, wu_hbm, wd_hbm,
     out_ref,
-    wg, wu, wd, send_a, send_b, send_c, recv_a, recv_b, recv_c, blocks_a, blocks_b, toks, gates, slot_ref,
+    x_ref, fresh_ref, wg, wu, wd, send_a, send_b, send_c, recv_a, recv_b, recv_c, blocks_a, blocks_b, toks, gates, slot_ref,
     tok_made, gate_made, slot_made,
     by_token, by_slot, rows_a, rows_b, inverse_ref, current, arrived,
-    w_sem, send_sem, recv_a_sem, recv_b_sem, recv_c_sem, relay_send_sem, relay_recv_sem,
+    row_sem, w_sem, send_sem, recv_a_sem, recv_b_sem, recv_c_sem, relay_send_sem, relay_recv_sem,
     block_send_sem, block_recv_sem, table_send_sem, table_recv_sem, made_sem, greet_sem,
 ):
     me = lax.axis_index("expert")
@@ -71,6 +72,14 @@
     def _():
         pl.semaphore_signal(barrier, inc=1, device_id=(section + 1, me), device_id_type=MESH)
 
+    row_copies = [
+        pltpu.make_async_copy(src, dst, row_sem.at[n])
+        for n, (src, dst) in enumerate(
+            ((x_hbm.at[0], x_ref.at[0]), (x_hbm.at[1], x_ref.at[1]), (fresh_hbm, fresh_ref))
+        )
+    ]
+    for copy in row_copies:
+        copy.start()
     weight_copies = [
         pltpu.make_async_copy(src, dst, w_sem.at[n])
         for n, (src, dst) in enumerate(((wg_hbm, wg), (wu_hbm, wu), (wd_hbm, wd)))
@@ -110,16 +119,24 @@
             device_id=(section, peer(me, 1, step)), device_id_type=MESH,
         )
 
-    def block_copies(kind, tick):
+    def start_blocks(kind, tick):
         blocks = (blocks_a, blocks_b)[kind][tick]
-        whole = pl.ds(0, TOK)
-        return [
-            along_z(
-                blocks[OWN].at[whole], blocks[side].at[whole],
-                block_send_sem.at[kind, tick, side - 1], block_recv_sem.at[kind, tick, side - 1], SHIFT[side],
-            )
-            for side in (BEHIND, AHEAD)
-        ]
+
+        def body(part, carry):
+            rows = pl.ds(part * PART_ROWS, PART_ROWS)
+            for side in (BEHIND, AHEAD):
+                along_z(
+                    blocks[OWN].at[rows], blocks[side].at[rows],
+                    block_send_sem.at[kind, tick, side - 1], block_recv_sem.at[kind, tick, side - 1], SHIFT[side],
+                ).start()
+            return carry
+
+        lax.fori_loop(0, TOK // PART_ROWS, body, 0)
+
+    def await_blocks(kind, tick):
+        blocks = (blocks_a, blocks_b)[kind][tick]
+        for side in (BEHIND, AHEAD):
+            wait_bytes(blocks[side].at[pl.ds(0, TOK)], block_recv_sem.at[kind, tick, side - 1])
 
     table_copies = [
         along_z(
@@ -334,9 +351,10 @@
 
     for i in ring_y:
         greet(greet_sem.at[0], i)
-    start(block_copies(1, 0))
+    start_blocks(1, 0)
+    row_copies[0].wait()
     load_normed(0)
-    start(block_copies(0, 0))
+    start_blocks(0, 0)
     make_tables()
     made_copies = [
         pltpu.make_async_copy(made, held, made_sem.at[n])
@@ -349,21 +367,22 @@
     for copy in made_copies:
         copy.wait()
     start(table_copies)
+    row_copies[1].wait()
     load_normed(1)
-    start(block_copies(0, 1))
+    start_blocks(0, 1)
     pl.semaphore_wait(greet_sem.at[1], 1)
     pack_own(1, 0)
     pack_own(0, 0)
     await_arrival(table_copies)
-    await_arrival(block_copies(1, 0))
+    await_blocks(1, 0)
     pack_sides(1, 0)
-    await_arrival(block_copies(0, 0))
+    await_blocks(0, 0)
     pack_sides(0, 0)
-    for copy in weight_copies:
+    for copy in (row_copies[2], *weight_copies):
         copy.wait()
     experts(0)
     pack_own(0, 1)
-    await_arrival(block_copies(0, 1))
+    await_blocks(0, 1)
     pack_sides(0, 1, 0, 2)
     combine(0)
 
@@ -383,14 +402,14 @@
         current[...] = fresh_ref[...]
 
     load_current(1)
-    start(block_copies(1, 1))
+    start_blocks(1, 1)
     pack_own(1, 1)
 
     @pl.when(~lower)
     def _():
         pack_sides(0, 1, 2, 4)
 
-    await_arrival(block_copies(1, 1))
+    await_blocks(1, 1)
     pack_sides(1, 1)
     experts(1)
     combine(1)
@@ -404,8 +423,9 @@
         copy.wait_send()
     for kind in range(2):
         for tick in range(TICKS):
-            for copy in block_copies(kind, tick):
-                copy.wait_send()
+            for side in (BEHIND, AHEAD):
+                own = (blocks_a, blocks_b)[kind][tick][OWN]
+                wait_bytes(own.at[pl.ds(0, TOK)], block_send_sem.at[kind, tick, side - 1])
     for kind, (sent, stayed) in enumerate(((send_a, 3), (send_b, 3), (send_c, 1))):
         for tick in range(TICKS):
             wait_bytes(sent.at[tick, pl.ds(stayed * SLOTS, ROWS - stayed * SLOTS)], send_sem.at[kind, tick])
@@ -420,9 +440,11 @@
     out = pl.pallas_call(
         kernel,
         out_shape=jax.ShapeDtypeStruct((TICKS, TOK, D), jnp.bfloat16),
-        in_specs=[vmem] * 6 + [hbm] * 3,
+        in_specs=[vmem] * 4 + [hbm] * 5,
         out_specs=vmem,
         scratch_shapes=[
+            pltpu.VMEM((TICKS, TOK, D), jnp.bfloat16),
+            pltpu.VMEM((TOK, D), jnp.bfloat16),
             pltpu.VMEM((D, FFE), jnp.bfloat16),
             pltpu.VMEM((D, FFE), jnp.bfloat16),
             pltpu.VMEM((FFE, D), jnp.bfloat16),
@@ -442,6 +464,7 @@
             pltpu.VMEM((TOK, D), jnp.bfloat16),
             pltpu.VMEM((TOK, D), jnp.bfloat16),
             pltpu.SemaphoreType.DMA((3,)),
+            pltpu.SemaphoreType.DMA((3,)),
             pltpu.SemaphoreType.DMA((3, TICKS)),
             pltpu.SemaphoreType.DMA((TICKS, GROUPS)),
             pltpu.SemaphoreType.DMA((TICKS, GROUPS)),
@@ -458,7 +481,7 @@
         compiler_params=pltpu.CompilerParams(
             collective_id=0, has_side_effects=True, vmem_limit_bytes=56 << 20
         ),
-    )(*by_choice, layer_input[:, 0], entering[0], fresh[0], norm_gain, w_gate[0, 0], w_up[0, 0], w_down[0, 0])
+    )(*by_choice, entering[0], norm_gain, layer_input[:, 0], fresh[0], w_gate[0, 0], w_up[0, 0], w_down[0, 0])
     return out[:, None]
 
 

time: 210 us -> 209 us (level)
  no operation moved by 1% of the time
where the time goes in v5:
time: 209 us
  Pallas kernels  206 us (99%)
  local copies, waits for them, and re-layouts  2.3 us (1%)
    pallas_call x1, Pallas kernels, local(): pl.pallas_call(kernel, out_shape=jax.ShapeDtypeStruct((TICKS, TOK, D), jn...  206 us

profile of v5, /device:TPU:1, one launch (start us, length us, event | category | flops | bytes accessed | tf_op | source)
XLA Modules:
  0.0 208.6 jit_solution(4690327989539847531)
XLA Ops:
  0.0 206.3 %shard_map.91 = bf16[2,128,2048]{2,1,0:T(8,128)(2,1)} custom-call(s32[2,2,128]{2,1,0:T(2,128)} %bitcast.22, bf16[2,2,128]{2,1,0:T(2,128)(2,1)} %bitcast.23, bf16[128,2048]{1,0:T(8,128)(2,1)} %bitcast.20, f32[1,2048]{1,0:T(1,128)} %gain_ref.1, bf16[2,128,2048]{2,1,0:T(8,128)(2,1)} %bitcast.19, bf16[128,2048]{1,0:T(8,128)(2,1)} %bitcast.21, ...), custom_call_target="tpu_custom_call" | custom-call | tf_op jit(solution)/shard_map/pallas_call | solution.py:440
  206.3 2.3 %copy.12 = bf16[2,1,128,2048]{3,2,1,0:T(8,128)(2,1)} copy(bf16[2,1,128,2048]{3,2,1,0:T(8,128)(2,1)} %bitcast.15) | data formatting | bytes 2097152
